TPU v7x, 512 devices: a whole 4x8x8 slice. The times are simulated.
512 devices in a mesh: tap: 64 (over y_hi, x, z), tm: 8 (over y_lo, core).
Axes of the slice: x: 4, y: 8 (y_hi: 2, y_lo: 4; y = y_hi * 4 + y_lo), z: 8, core: 2. Of those that a mesh axis runs over, the one named last changes fastest.
Arguments:
- pressure: bfloat16 [2048, 8192], P('tap', 'tm'), may hold values from -12 to 12
- filters: float32 [2, 16], replicated, may hold values from -1.5 to 1.5
Outputs:
- scalograms: float32 [3, 2048, 2048], P(None, 'tap', 'tm')
All inputs are finite; a program needn't handle non-finite values.
Results may differ from a plain program's by a relative error of at most 0.0003.
Values may be sent and summed in bfloat16 or wider, within the bound.
A program may use at most 128 MiB of HBM per device.

v0:
```python
import jax
import jax.numpy as jnp
from jax import lax
from jax.sharding import PartitionSpec as P

FILT = 16
LEVELS = 3


def extended_2(block, sides, width):
    for axis, dim in sides:
        count = lax.axis_size(axis)
        forward = [(i, i + 1) for i in range(count - 1)]
        forward.append((count - 1, 0))
        backward = [(target, source) for source, target in forward]
        low = lax.ppermute(
            lax.slice_in_dim(block, block.shape[dim] - width, None, axis=dim), axis, forward
        )
        high = lax.ppermute(lax.slice_in_dim(block, 0, width, axis=dim), axis, backward)
        block = jnp.concatenate([low, block, high], axis=dim)
    return block


def levels_stepwise(pressure, filters):
    centre = FILT // 2
    width = pressure.shape[1]
    series = pressure.astype(jnp.float32)
    details = []
    for level_index in range(LEVELS):
        dilation = 2**level_index
        extended = extended_2(series, (("tm", 1),), centre * dilation)
        detail = jnp.zeros(series.shape, jnp.float32)
        for offset in range(FILT):
            first_col = offset * dilation
            detail = detail + filters[0, offset] * extended[:, first_col : first_col + width]
        details.append(detail.astype(jnp.bfloat16))
        if level_index + 1 < LEVELS:
            smooth = jnp.zeros(series.shape, jnp.float32)
            for offset in range(FILT):
                first_col = offset * dilation
                smooth = smooth + filters[1, offset] * extended[:, first_col : first_col + width]
            series = smooth
    return jnp.stack(details)


def cross_of(own_coeffs, arrived):
    return jnp.einsum("lpt,lqt->lpq", own_coeffs, arrived, preferred_element_type=jnp.float32)


def place_tile(own_coeffs, arrived):
    cross_tile = cross_of(own_coeffs, arrived)
    return cross_tile


def body(pressure, filters):
    width = pressure.shape[1]
    own_coeffs = levels_stepwise(pressure, filters)
    tiles = place_tile(own_coeffs, lax.all_gather(own_coeffs, "tap", axis=1, tiled=True))
    summed = lax.psum_scatter(tiles, "tm", scatter_dimension=2, tiled=True)
    samples_total = width * lax.axis_size("tm")
    return summed * (1.0 / samples_total)


def solution(mesh):
    placed = (P("tap", "tm"), P())
    return jax.shard_map(
        body, mesh=mesh, in_specs=placed, out_specs=P(None, "tap", "tm"), check_vma=False
    )
```

profile of v0, /device:TPU:2, one launch (start us, length us, event | category | flops | bytes accessed | tf_op | source)
XLA Modules:
  0.0 375.8 jit_solution(2376206812153674483)
XLA Ops:
  6.5 0.0 all-gather.2.cloned.1.call-start
  6.5 0.8 fusion.76
  7.3 4.9 %collective-permute-start.1 = (f32[32,8]{1,0:T(8,128)S(1)}, f32[32,8]{1,0:T(8,128)S(1)}, u32[]{:S(2)}, u32[]{:S(2)}) collective-permute-start(f32[32,8]{1,0:T(8,128)S(1)} %get-tuple-element.9), channel_id=1, source_target_pairs={{1,0},{2,1},{3,2},{4,3},{5,4},{6,5},{7,6},{0,7},{9,8},{10,9},{11,1... | collective-permute-start | bytes 3080 | tf_op jit(solution)/shard_map/ppermute | solution.py:19
  12.3 1.9 collective-permute-start
  14.2 2.1 fusion.77
  16.3 1.9 fusion.78
  18.2 0.8 convert_element_type.12
  19.0 0.0 collective-permute-done.1
  19.0 0.1 collective-permute-done
  19.1 10.5 %multiply_add_fusion.1 = f32[32,1024]{1,0:T(8,128)S(1)} fusion(f32[32,1024]{1,0:T(8,128)S(1)} %convert_element_type.12, f32[32,8]{1,0:T(8,128)S(1)} %collective-permute-done, f32[32,8]{1,0:T(8,128)S(1)} %collective-permute-done.1, f32[]{:T(128)} %bitcast.32, f32[]{:T(128)} %bitcast.31, f32[]{:T(128)} %bitcast.30, f32[]{:T(128)} %bitcast.29, f32[]{:T(128)} %bitcast.28, ...), kind=kLoop, calls=%fused_computation.156 | loop fusion | flops 1507328 | bytes 264256 | tf_op jit(solution)/shard_map/add | solution.py:41
  29.7 0.1 fusion.75
  29.7 5.3 %collective-permute-start.3 = (f32[32,16]{1,0:T(8,128)S(1)}, f32[32,16]{1,0:T(8,128)S(1)}, u32[]{:S(2)}, u32[]{:S(2)}) collective-permute-start(f32[32,16]{1,0:T(8,128)S(1)} %get-tuple-element.7), channel_id=1, source_target_pairs={{1,0},{2,1},{3,2},{4,3},{5,4},{6,5},{7,6},{0,7},{9,8},{10,9},{11,1... | collective-permute-start | bytes 6152 | tf_op jit(solution)/shard_map/ppermute | solution.py:19
  35.1 1.9 collective-permute-start.2
  37.0 10.8 %fusion.70 = bf16[1,32,1024]{2,1,0:T(8,128)(2,1)S(1)} fusion(f32[32,8]{1,0:T(8,128)S(1)} %collective-permute-done.1, f32[32,1024]{1,0:T(8,128)S(1)} %convert_element_type.12, f32[]{:T(128)} %bitcast.15, f32[]{:T(128)} %bitcast.14, f32[]{:T(128)} %bitcast.13, f32[]{:T(128)} %bitcast.12, f32[]{:T(128)} %bitcast.11, f32[]{:T(128)} %bitcast.10, f32[]{:T(128)} %bitcast.9, ...), kind=kLoop, calls=%fused_computation.159 | loop fusion | flops 1540096 | bytes 198720 | tf_op jit(solution)/shard_map/stack | solution.py:43
  47.8 0.0 collective-permute-done.3
  47.8 0.0 collective-permute-done.2
  47.8 10.5 %multiply_add_fusion = f32[32,1024]{1,0:T(8,128)S(1)} fusion(f32[32,1024]{1,0:T(8,128)S(1)} %multiply_add_fusion.1, f32[32,16]{1,0:T(8,128)S(1)} %collective-permute-done.2, f32[32,16]{1,0:T(8,128)S(1)} %collective-permute-done.3, f32[]{:T(128)} %bitcast.32, f32[]{:T(128)} %bitcast.31, f32[]{:T(128)} %bitcast.30, f32[]{:T(128)} %bitcast.29, f32[]{:T(128)} %bitcast.28, ...), kind=kLoop, calls=%fused_computation.154 | loop fusion | flops 1507328 | bytes 266304 | tf_op jit(solution)/shard_map/add | solution.py:41
  58.3 0.1 fusion.74
  58.4 1.9 collective-permute-start.4
  60.3 5.4 %collective-permute-start.5 = (f32[32,32]{1,0:T(8,128)S(1)}, f32[32,32]{1,0:T(8,128)S(1)}, u32[]{:S(2)}, u32[]{:S(2)}) collective-permute-start(f32[32,32]{1,0:T(8,128)S(1)} %get-tuple-element.6), channel_id=1, source_target_pairs={{1,0},{2,1},{3,2},{4,3},{5,4},{6,5},{7,6},{0,7},{9,8},{10,9},{11,1... | collective-permute-start | bytes 12296 | tf_op jit(solution)/shard_map/ppermute | solution.py:19
  65.8 10.8 %fusion.71 = bf16[1,32,1024]{2,1,0:T(8,128)(2,1)S(1)} fusion(f32[32,16]{1,0:T(8,128)S(1)} %collective-permute-done.3, f32[32,1024]{1,0:T(8,128)S(1)} %multiply_add_fusion.1, f32[]{:T(128)} %bitcast.15, f32[]{:T(128)} %bitcast.14, f32[]{:T(128)} %bitcast.13, f32[]{:T(128)} %bitcast.12, f32[]{:T(128)} %bitcast.11, f32[]{:T(128)} %bitcast.10, f32[]{:T(128)} %bitcast.9, ...), kind=kLoop, calls=%fused_computation.160 | loop fusion | flops 1540096 | bytes 200768 | tf_op jit(solution)/shard_map/stack | solution.py:43
  76.5 0.0 collective-permute-done.4
  76.5 0.0 collective-permute-done.5
  76.5 10.8 %fusion.72 = bf16[1,32,1024]{2,1,0:T(8,128)(2,1)S(1)} fusion(f32[32,32]{1,0:T(8,128)S(1)} %collective-permute-done.5, f32[32,1024]{1,0:T(8,128)S(1)} %multiply_add_fusion, f32[]{:T(128)} %bitcast.15, f32[]{:T(128)} %bitcast.14, f32[]{:T(128)} %bitcast.13, f32[]{:T(128)} %bitcast.12, f32[]{:T(128)} %bitcast.11, f32[]{:T(128)} %bitcast.10, f32[]{:T(128)} %bitcast.9, ...), kind=kLoop, calls=%fused_computation.161 | loop fusion | flops 1540096 | bytes 204864 | tf_op jit(solution)/shard_map/stack | solution.py:43
  87.3 0.7 pad_maximum_fusion
  88.0 0.0 all-gather.2.cloned.1.call-update
  88.0 0.0 reduce-scatter.2.cloned.1.call-start
  88.1 237.1 %all-gather.2.cloned.1.call-done = bf16[3,2048,1024]{2,1,0:T(8,128)(2,1)} async-done(((bf16[3,32,1024]{2,1,0:T(8,128)(2,1)}), bf16[3,2048,1024]{2,1,0:T(8,128)(2,1)}) %all-gather.2.cloned.1.call-update) | async-done | bytes 12582928 | tf_op jit(solution)/shard_map/all_gather | solution.py:58
  325.2 9.3 %fusion.73 = f32[3,32,2048]{2,1,0:T(8,128)} fusion(bf16[3,2048,1024]{2,1,0:T(8,128)(2,1)} %all-gather.2.cloned.1.call-done, bf16[1,32,1024]{2,1,0:T(8,128)(2,1)S(1)} %fusion.72, bf16[1,32,1024]{2,1,0:T(8,128)(2,1)S(1)} %fusion.71, bf16[1,32,1024]{2,1,0:T(8,128)(2,1)S(1)} %fusion.70), kind=kOutput, calls=%fused_computation.163 | convolution fusion | flops 402849792 | bytes 13565952 | tf_op jit(solution)/shard_map/lpt,lqt->lpq/dot_general | solution.py:47
  334.5 0.0 reduce-scatter.2.cloned.1.call-update
  334.5 32.9 %reduce-scatter.2.cloned.1.call-done = f32[3,32,256]{2,1,0:T(8,128)} async-done(((f32[3,32,2048]{2,1,0:T(8,128)}), f32[3,32,256]{2,1,0:T(8,128)}) %reduce-scatter.2.cloned.1.call-update) | async-done | bytes 98320 | tf_op jit(solution)/shard_map/reduce_scatter | solution.py:59
  367.4 1.5 broadcast_multiply_fusion
Async XLA Ops:
  6.5 318.6 %all-gather.2.cloned.1.call-start = ((), (), s32[]{:S(2)}) async-start(), calls=%async_computation.1 | async-start | bytes 12779520 | tf_op jit(solution)/shard_map/all_gather | solution.py:58
  7.3 11.7 %collective-permute-start.1 = (f32[32,8]{1,0:T(8,128)S(1)}, f32[32,8]{1,0:T(8,128)S(1)}, u32[]{:S(2)}, u32[]{:S(2)}) collective-permute-start(f32[32,8]{1,0:T(8,128)S(1)} %get-tuple-element.9), channel_id=1, source_target_pairs={{1,0},{2,1},{3,2},{4,3},{5,4},{6,5},{7,6},{0,7},{9,8},{10,9},{11,1... | collective-permute-start | bytes 3080 | tf_op jit(solution)/shard_map/ppermute | solution.py:19
  12.3 6.9 %collective-permute-start = (f32[32,8]{1,0:T(8,128)S(1)}, f32[32,8]{1,0:T(8,128)S(1)}, u32[]{:S(2)}, u32[]{:S(2)}) collective-permute-start(f32[32,8]{1,0:T(8,128)S(1)} %get-tuple-element.10), channel_id=1, source_target_pairs={{0,1},{1,2},{2,3},{3,4},{4,5},{5,6},{6,7},{7,0},{8,9},{9,10},{10,1... | collective-permute-start | bytes 3080 | tf_op jit(solution)/shard_map/ppermute | solution.py:16
  29.7 18.0 %collective-permute-start.3 = (f32[32,16]{1,0:T(8,128)S(1)}, f32[32,16]{1,0:T(8,128)S(1)}, u32[]{:S(2)}, u32[]{:S(2)}) collective-permute-start(f32[32,16]{1,0:T(8,128)S(1)} %get-tuple-element.7), channel_id=1, source_target_pairs={{1,0},{2,1},{3,2},{4,3},{5,4},{6,5},{7,6},{0,7},{9,8},{10,9},{11,1... | collective-permute-start | bytes 6152 | tf_op jit(solution)/shard_map/ppermute | solution.py:19
  35.1 12.7 %collective-permute-start.2 = (f32[32,16]{1,0:T(8,128)S(1)}, f32[32,16]{1,0:T(8,128)S(1)}, u32[]{:S(2)}, u32[]{:S(2)}) collective-permute-start(f32[32,16]{1,0:T(8,128)S(1)} %get-tuple-element.8), channel_id=1, source_target_pairs={{0,1},{1,2},{2,3},{3,4},{4,5},{5,6},{6,7},{7,0},{8,9},{9,10},{10,1... | collective-permute-start | bytes 6152 | tf_op jit(solution)/shard_map/ppermute | solution.py:16
  58.4 18.1 %collective-permute-start.4 = (f32[32,32]{1,0:T(8,128)S(1)}, f32[32,32]{1,0:T(8,128)S(1)}, u32[]{:S(2)}, u32[]{:S(2)}) collective-permute-start(f32[32,32]{1,0:T(8,128)S(1)} %get-tuple-element.5), channel_id=1, source_target_pairs={{0,1},{1,2},{2,3},{3,4},{4,5},{5,6},{6,7},{7,0},{8,9},{9,10},{10,1... | collective-permute-start | bytes 12296 | tf_op jit(solution)/shard_map/ppermute | solution.py:16
  60.3 16.2 %collective-permute-start.5 = (f32[32,32]{1,0:T(8,128)S(1)}, f32[32,32]{1,0:T(8,128)S(1)}, u32[]{:S(2)}, u32[]{:S(2)}) collective-permute-start(f32[32,32]{1,0:T(8,128)S(1)} %get-tuple-element.6), channel_id=1, source_target_pairs={{1,0},{2,1},{3,2},{4,3},{5,4},{6,5},{7,6},{0,7},{9,8},{10,9},{11,1... | collective-permute-start | bytes 12296 | tf_op jit(solution)/shard_map/ppermute | solution.py:19
  88.0 279.4 %reduce-scatter.2.cloned.1.call-start = ((), (), s32[]{:S(2)}) async-start(), calls=%async_computation.2 | async-start | bytes 884736 | tf_op jit(solution)/shard_map/reduce_scatter | solution.py:59
Sparse Core Ops, SparseCore 0:
  88.1 236.9 all-gather.1
  334.7 32.7 reduce-scatter.1
where the time goes:
time: 377 us; the launch traced here: 376 us
  waiting for transfers between devices  270 us (72%)
  other arithmetic  56.4 us (15%)
  starting transfers between devices  21.5 us (6%)
  between operations  13.5 us (4%)
  matrix products  9.33 us (2%)
  local copies, waits for them, and re-layouts  4.9 us (1%)
    all_gather x1, waiting for transfers between devices, body(): lax.all_gather(own_coeffs, 'tap', axis=1, tiled=True)  237 us
    another operation x4, other arithmetic, levels_stepwise(): return jnp.stack(details)  32.9 us
    reduce_scatter x1, waiting for transfers between devices, body(): summed = lax.psum_scatter(tiles, 'tm', scatter_dimension=2, tiled=True)  32.9 us
    add x2, other arithmetic, levels_stepwise(): smooth + filters[1, offset] * extended[:, first_col:first_col + width]  21.1 us
    ppermute x3, starting transfers between devices, extended_2(): lax.ppermute(lax.slice_in_dim(block, 0, width, axis=dim), axis, backward)  15.7 us
    dot_general x1, matrix products, cross_of(): jnp.einsum('lpt,lqt->lpq', own_coeffs, arrived, preferred_element_type=jn...  9.33 us
  transfers between devices with their start and end apart: 8, of which 3 were waited for; matrix products, arithmetic and copies ran while one was open for 7% of the time, Pallas kernels for 0%

commit v1 on v0

v1 whole, which is shorter than its diff:
```python
import jax
import jax.numpy as jnp
from jax import lax
from jax.experimental import pallas as pl
from jax.experimental.pallas import tpu as pltpu
from jax.sharding import PartitionSpec as P

FILT = 16
LEVELS = 3
NX, NZ, NYH, NYL = 4, 8, 2, 4
ROWS = 32
WIDTH = 1024
HALO = 128
EXT = WIDTH + HALO
WIN = 256
OUT = 128
NWIN = WIDTH // OUT
SPLITS = 3
LANES = 384
MESH = pl.DeviceIdType.MESH
NT = (((1,), (1,)), ((), ()))


def remote(src, dst, send, recv, tap, tm):
    return pltpu.make_async_remote_copy(
        src_ref=src, dst_ref=dst, send_sem=send, recv_sem=recv,
        device_id=(tap, tm), device_id_type=MESH,
    )


def build_bands(f_ref, wbuf):
    lane = lax.broadcasted_iota(jnp.int32, (8, LANES), 1)

    def comb(row, top, step):
        line = jnp.zeros((8, LANES), jnp.float32)
        for k in range(FILT):
            line = jnp.where(lane == top - step * k, f_ref[row, k], line)
        return line

    def smoothed(line, step):
        total = jnp.zeros((8, LANES), jnp.float32)
        for k in range(FILT):
            moved = line if k == 0 else pltpu.roll(line, LANES - step * k, 1)
            total = total + f_ref[1, k] * moved
        return total

    lines = [
        comb(0, 328, 1),
        smoothed(comb(0, 344, 2), 1),
        smoothed(smoothed(comb(0, 376, 4), 2), 1),
    ]
    for level, line in enumerate(lines):
        wide = jnp.broadcast_to(line[0:1, :], (WIN, LANES))
        band = pltpu.roll(wide, 0, 1, stride=1, stride_axis=0)[:, :OUT]
        for piece in range(SPLITS):
            part = band.astype(jnp.bfloat16)
            wbuf[piece, :, level * OUT : (level + 1) * OUT] = part
            band = band - part.astype(jnp.float32)


def details_of(rows_ext, wbuf):
    windows = jnp.concatenate(
        [rows_ext[:, w * OUT : w * OUT + WIN] for w in range(NWIN)], axis=0
    )
    total = jnp.dot(windows, wbuf[0], preferred_element_type=jnp.float32)
    for piece in range(1, SPLITS):
        total += jnp.dot(windows, wbuf[piece], preferred_element_type=jnp.float32)
    return total.astype(jnp.bfloat16)


def kernel(
    p_ref, f_ref, o_ref,
    pbuf, qbuf, wbuf, dp, dq, part, sib, red, xo, yo,
    hs, hr, xs, xr, cs, cr, zps, zpr, zms, zmr, ss, sr, xos, xor_, yos, yor,
):
    a = lax.axis_index("tap")
    b = lax.axis_index("tm")
    y_hi = a // (NX * NZ)
    x = (a // NZ) % NX
    z = a % NZ
    y_lo = b // 2
    core = b % 2

    def tap_of(yh, xx, zz):
        return yh * (NX * NZ) + xx * NZ + zz

    b_next = (b + 1) % 8
    b_prev = (b + 7) % 8
    home = y_hi == x // 2
    far_x = 2 * y_hi + x // 2
    far_tap = tap_of(1 - y_hi, far_x, z)
    z_up = tap_of(y_hi, x, (z + 1) % NZ)
    z_down = tap_of(y_hi, x, (z + NZ - 1) % NZ)
    sibling = y_lo * 2 + (1 - core)

    barrier = pltpu.get_barrier_semaphore()

    def hello(tap, tm):
        pl.semaphore_signal(barrier, inc=1, device_id=(tap, tm), device_id_type=MESH)

    hello(a, b_next)
    hello(a, b_prev)
    for d in range(1, 4):
        hello(a, (b + 2 * d) % 8)
        hello(tap_of(y_hi, (x + d) % NX, z), b)
    hello(z_up, b)
    hello(z_down, b)
    hello(far_tap, b)

    @pl.when(jnp.logical_not(home))
    def _():
        for s in range(2):
            hello(tap_of(1 - y_hi, 2 * (x % 2) + s, z), b)

    pbuf[x, :, 0:WIDTH] = p_ref[...]
    pl.semaphore_wait(barrier, jnp.where(home, 11, 13))

    halo = remote(
        p_ref.at[:, pl.ds(0, HALO)], pbuf.at[x, :, pl.ds(WIDTH, HALO)],
        hs.at[0], hr.at[0], a, b_prev,
    )
    halo.start()
    build_bands(f_ref, wbuf)
    halo.wait_recv()

    cross = remote(pbuf.at[x], qbuf.at[z, x % 2], cs.at[0], cr.at[x % 2], far_tap, b)
    cross.start()
    ring = []
    for d in range(1, 4):
        ring.append(remote(
            pbuf.at[x], pbuf.at[x], xs.at[d - 1], xr.at[d - 1],
            tap_of(y_hi, (x + d) % NX, z), b,
        ))
        ring[-1].start()
    for d in range(1, 4):
        slot = pbuf.at[(x + NX - d) % NX]
        remote(slot, slot, xs.at[d - 1], xr.at[d - 1], z_up, b).wait_recv()

    @pl.when(home)
    def _():
        for s in range(2):
            qbuf[z, s] = pbuf[2 * (x % 2) + s]

    @pl.when(jnp.logical_not(home))
    def _():
        for s in range(2):
            slot = qbuf.at[z, s]
            remote(slot, slot, cs.at[0], cr.at[s], far_tap, b).wait_recv()

    sends = [halo, cross] + ring

    def up(k, s):
        slot = qbuf.at[(z + NZ - k) % NZ, s]
        sends.append(remote(slot, slot, zps.at[2 * k + s], zpr.at[2 * k + s], z_up, b))
        sends[-1].start()

    def down(k, s):
        slot = qbuf.at[(z + k) % NZ, s]
        sends.append(remote(slot, slot, zms.at[2 * k + s], zmr.at[2 * k + s], z_down, b))
        sends[-1].start()

    def from_below(k, s):
        slot = qbuf.at[(z + 2 * NZ - 1 - k) % NZ, s]
        remote(slot, slot, zps.at[2 * k + s], zpr.at[2 * k + s], z_up, b).wait_recv()

    def from_above(k, s):
        slot = qbuf.at[(z + 1 + k) % NZ, s]
        remote(slot, slot, zms.at[2 * k + s], zmr.at[2 * k + s], z_down, b).wait_recv()

    def columns(m):
        zz = (z + m) % NZ
        ext = jnp.concatenate([qbuf[zz, 0], qbuf[zz, 1]], axis=0)
        val = details_of(ext, wbuf)
        for w in range(NWIN):
            for s in range(2):
                first = w * 2 * ROWS + s * ROWS
                for j in range(LEVELS):
                    dq[j, s * 256 + m * ROWS : s * 256 + (m + 1) * ROWS, w * OUT : (w + 1) * OUT] = (
                        val[first : first + ROWS, j * OUT : (j + 1) * OUT]
                    )

    for s in range(2):
        up(0, s)
        down(0, s)

    rows_ext = jnp.concatenate([pbuf[i] for i in range(NX)], axis=0)
    val = details_of(rows_ext, wbuf)
    for w in range(NWIN):
        for j in range(LEVELS):
            dp[j, :, w * OUT : (w + 1) * OUT] = val[
                w * NX * ROWS : (w + 1) * NX * ROWS, j * OUT : (j + 1) * OUT
            ]
    columns(0)
    for k in range(3):
        for s in range(2):
            from_below(k, s)
            if k < 2 or s == 0:
                up(k + 1, s)
            from_above(k, s)
            if k < 2 or s == 1:
                down(k + 1, s)
        columns(1 + k)
        columns(7 - k)
    from_below(3, 0)
    from_above(3, 1)
    columns(4)

    for j in range(LEVELS):
        prod = lax.dot_general(dp[j], dq[j], NT, preferred_element_type=jnp.float32)
        for s in range(2):
            part[s, j] = prod[:, s * 256 : (s + 1) * 256]

    pair = remote(part.at[1 - core], sib, ss.at[0], sr.at[0], a, sibling)
    pair.start()
    pair.wait_recv()
    sends.append(pair)
    for i in range(NX):
        for j in range(LEVELS):
            red[i, j] = part[core, j, i * ROWS : (i + 1) * ROWS] + sib[j, i * ROWS : (i + 1) * ROWS]

    for d in range(1, 4):
        there = (x + d) % NX
        sends.append(remote(
            red.at[there], xo.at[x], xos.at[d - 1], xor_.at[d - 1], tap_of(y_hi, there, z), b
        ))
        sends[-1].start()
    xo[x] = red[x]
    for d in range(1, 4):
        slot = xo.at[(x + NX - d) % NX]
        remote(slot, slot, xos.at[d - 1], xor_.at[d - 1], z_up, b).wait_recv()

    for d in range(1, 4):
        there = (y_lo + d) % NYL
        sends.append(remote(
            xo.at[there], yo.at[d - 1], yos.at[d - 1], yor.at[d - 1], a, there * 2 + core
        ))
        sends[-1].start()
    total = xo[y_lo]
    for d in range(1, 4):
        slot = yo.at[d - 1]
        remote(slot, slot, yos.at[d - 1], yor.at[d - 1], a, sibling).wait_recv()
    total = total + (yo[0] + yo[1] + yo[2])
    total = total * (1.0 / (WIDTH * 8))
    for j in range(LEVELS):
        o_ref[j] = pltpu.roll(total[j], z * ROWS, 1)
    for copy in sends:
        copy.wait_send()


def body(pressure, filters):
    dma = pltpu.SemaphoreType.DMA
    return pl.pallas_call(
        kernel,
        out_shape=jax.ShapeDtypeStruct((LEVELS, ROWS, 256), jnp.float32),
        in_specs=[
            pl.BlockSpec(memory_space=pltpu.VMEM),
            pl.BlockSpec(memory_space=pltpu.SMEM),
        ],
        out_specs=pl.BlockSpec(memory_space=pltpu.VMEM),
        scratch_shapes=[
            pltpu.VMEM((NX, ROWS, EXT), jnp.bfloat16),
            pltpu.VMEM((NZ, 2, ROWS, EXT), jnp.bfloat16),
            pltpu.VMEM((SPLITS, WIN, LEVELS * OUT), jnp.bfloat16),
            pltpu.VMEM((LEVELS, NX * ROWS, WIDTH), jnp.bfloat16),
            pltpu.VMEM((LEVELS, 512, WIDTH), jnp.bfloat16),
            pltpu.VMEM((2, LEVELS, NX * ROWS, 256), jnp.float32),
            pltpu.VMEM((LEVELS, NX * ROWS, 256), jnp.float32),
            pltpu.VMEM((NX, LEVELS, ROWS, 256), jnp.float32),
            pltpu.VMEM((NX, LEVELS, ROWS, 256), jnp.float32),
            pltpu.VMEM((3, LEVELS, ROWS, 256), jnp.float32),
            dma((1,)), dma((1,)),
            dma((3,)), dma((3,)),
            dma((1,)), dma((2,)),
            dma((8,)), dma((8,)),
            dma((8,)), dma((8,)),
            dma((1,)), dma((1,)),
            dma((3,)), dma((3,)),
            dma((3,)), dma((3,)),
        ],
        compiler_params=pltpu.CompilerParams(
            collective_id=0, has_side_effects=True, vmem_limit_bytes=40 * 1024 * 1024
        ),
        cost_estimate=pl.CostEstimate(
            flops=4_000_000_000, bytes_accessed=200_000, transcendentals=0
        ),
    )(pressure, filters)


def solution(mesh):
    placed = (P("tap", "tm"), P())
    return jax.shard_map(
        body, mesh=mesh, in_specs=placed, out_specs=P(None, "tap", "tm"), check_vma=False
    )
```

time: 377 us -> 62.4 us (0.17)
  the two profiles are of different devices: /device:TPU:2 before, /device:TPU:8 now
where the time goes in v1:
time: 62.4 us; the launch traced here: 62.2 us
  Pallas kernels  60 us (96%)
  local copies, waits for them, and re-layouts  2.16 us (3%)
    pallas_call x1, Pallas kernels, body(): pl.pallas_call(kernel, out_shape=jax.ShapeDtypeStruct((LEVELS, ROWS, 256)...  60 us
    unnamed x5, local copies, waits for them, and re-layouts  2.16 us

profile of v1, /device:TPU:8, one launch (start us, length us, event | category | flops | bytes accessed | tf_op | source)
XLA Modules:
  0.0 62.2 jit_solution(1129970657938935379)
XLA Ops:
  0.0 0.0 copy-start
  0.0 0.8 %copy-done = bf16[32,1024]{1,0:T(8,128)(2,1)S(1)} copy-done((bf16[32,1024]{1,0:T(8,128)(2,1)S(1)}, bf16[32,1024]{1,0:T(8,128)(2,1)}, u32[]{:S(2)}) %copy-start) | copy-done | bytes 65560
  0.8 0.0 copy-start.1
  0.8 0.7 %copy-done.1 = f32[2,16]{1,0:T(2,128)S(1)} copy-done((f32[2,16]{1,0:T(2,128)S(1)}, f32[2,16]{1,0:T(2,128)}, u32[]{:S(2)}) %copy-start.1) | copy-done | bytes 152
  1.5 60.0 %shard_map.28 = f32[3,32,256]{2,1,0:T(8,128)S(1)} custom-call(bf16[32,1024]{1,0:T(8,128)(2,1)S(1)} %copy-done, f32[2,16]{1,0:T(2,128)S(1)} %copy-done.1), custom_call_target="tpu_custom_call" | custom-call | flops 4000000000 | bytes 200000 | tf_op jit(solution)/shard_map/pallas_call | solution.py:252
  61.5 0.6 %copy.4 = f32[3,32,256]{2,1,0:T(8,128)} copy(f32[3,32,256]{2,1,0:T(8,128)S(1)} %shard_map.28) | data formatting | bytes 196608
Async XLA Ops:
  0.0 0.8 %copy-start = (bf16[32,1024]{1,0:T(8,128)(2,1)S(1)}, bf16[32,1024]{1,0:T(8,128)(2,1)}, u32[]{:S(2)}) copy-start(bf16[32,1024]{1,0:T(8,128)(2,1)} %p_ref.1) | copy-start | bytes 196612
  0.8 0.7 %copy-start.1 = (f32[2,16]{1,0:T(2,128)S(1)}, f32[2,16]{1,0:T(2,128)}, u32[]{:S(2)}) copy-start(f32[2,16]{1,0:T(2,128)} %f_ref.1) | copy-start | bytes 388

commit v2 on v1

v2 whole, which is shorter than its diff:
```python
import jax
import jax.numpy as jnp
from jax import lax
from jax.experimental import pallas as pl
from jax.experimental.pallas import tpu as pltpu
from jax.sharding import PartitionSpec as P

FILT = 16
LEVELS = 3
NX, NZ, NYL = 4, 8, 4
ROWS = 32
WIDTH = 1024
HALO = 128
WIN = 256
OUT = 128
NWIN = WIDTH // OUT
SPLITS = 3
LANES = 384
CHUNKS = 4
HALF = 16
PIECE = {1: (0, 0), 7: (0, 1), 2: (1, 0), 6: (1, 1), 3: (2, 0), 5: (2, 1), 0: (3, 0), 4: (3, 1)}
MESH = pl.DeviceIdType.MESH
NT = (((1,), (1,)), ((), ()))


def remote(src, dst, send, recv, tap, tm):
    return pltpu.make_async_remote_copy(
        src_ref=src, dst_ref=dst, send_sem=send, recv_sem=recv,
        device_id=(tap, tm), device_id_type=MESH,
    )


def build_bands(f_ref, wbuf):
    lane = lax.broadcasted_iota(jnp.int32, (8, LANES), 1)

    def comb(row, top, step):
        line = jnp.zeros((8, LANES), jnp.float32)
        for k in range(FILT):
            line = jnp.where(lane == top - step * k, f_ref[row, k], line)
        return line

    def smoothed(line, step):
        total = jnp.zeros((8, LANES), jnp.float32)
        for k in range(FILT):
            moved = line if k == 0 else pltpu.roll(line, LANES - step * k, 1)
            total = total + f_ref[1, k] * moved
        return total

    lines = [
        comb(0, 328, 1),
        smoothed(comb(0, 344, 2), 1),
        smoothed(smoothed(comb(0, 376, 4), 2), 1),
    ]
    for level, line in enumerate(lines):
        wide = jnp.broadcast_to(line[0:1, :], (WIN, LANES))
        band = pltpu.roll(wide, 0, 1, stride=1, stride_axis=0)[:, :OUT]
        for piece in range(SPLITS):
            part = band.astype(jnp.bfloat16)
            wbuf[piece, :, level * OUT : (level + 1) * OUT] = part
            band = band - part.astype(jnp.float32)


def details_of(main, halo, wbuf):
    ext = jnp.concatenate([main, halo], axis=1)
    windows = jnp.concatenate([ext[:, w * OUT : w * OUT + WIN] for w in range(NWIN)], axis=0)
    total = jnp.dot(windows, wbuf[0], preferred_element_type=jnp.float32)
    for piece in range(1, SPLITS):
        total += jnp.dot(windows, wbuf[piece], preferred_element_type=jnp.float32)
    return total.astype(jnp.bfloat16)


def kernel(
    p_ref, f_ref, o_ref,
    pbuf, hp, qbuf, hq, wbuf, dp, dq, part, sib, red, xo, yo, fin,
    hs, hr, xs, xr, xhs, xhr, cs, cr, chs, chr_, zus, zur, zds, zdr, zhus, zhur, zhds, zhdr,
    ss, sr, xos, xor_, yos, yor, fs, fr,
):
    a = lax.axis_index("tap")
    b = lax.axis_index("tm")
    y_hi = a // (NX * NZ)
    x = (a // NZ) % NX
    z = a % NZ
    y_lo = b // 2
    core = b % 2

    def tap_of(yh, xx, zz):
        return yh * (NX * NZ) + xx * NZ + zz

    b_next = (b + 1) % 8
    b_prev = (b + 7) % 8
    home = x % 2 == 0
    away = x % 2 == 1
    post = x // 2 == core
    far_tap = tap_of(1 - y_hi, 2 * (x // 2) + 1, z)
    z_up = tap_of(y_hi, x, (z + 1) % NZ)
    z_down = tap_of(y_hi, x, (z + NZ - 1) % NZ)
    sibling = y_lo * 2 + (1 - core)

    barrier = pltpu.get_barrier_semaphore()

    def hello(tap, tm):
        pl.semaphore_signal(barrier, inc=1, device_id=(tap, tm), device_id_type=MESH)

    hello(z_up, b)
    hello(z_down, b)
    hello(far_tap, b)

    @pl.when(away)
    def _():
        hello(tap_of(1 - y_hi, x - 1, z), b)

    hello(a, b_next)
    hello(a, b_prev)
    for d in range(1, 4):
        hello(a, (b + 2 * d) % 8)
        hello(tap_of(y_hi, (x + d) % NX, z), b)

    build_bands(f_ref, wbuf)
    pbuf[x] = p_ref[...]

    @pl.when(home)
    def _():
        qbuf[z, 0] = p_ref[...]

    pl.semaphore_wait(barrier, jnp.where(home, 11, 12))

    def far_copy(h):
        rows = pl.ds(h * HALF, HALF)
        return remote(
            p_ref.at[rows], qbuf.at[z, x % 2, rows], cs.at[h], cr.at[2 * (x % 2) + h], far_tap, b
        )

    sends = []

    def go(copy):
        copy.start()
        sends.append(copy)

    go(remote(p_ref.at[:, pl.ds(0, HALO)], hp.at[x], hs.at[0], hr.at[0], a, b_prev))
    for h in range(2):
        go(far_copy(h))
    for d in (3, 1, 2):
        go(remote(
            p_ref, pbuf.at[x], xs.at[d - 1], xr.at[d - 1], tap_of(y_hi, (x + d) % NX, z), b
        ))

    def chunk_of(zz, c):
        return qbuf.at[zz, c // 2, pl.ds((c % 2) * HALF, HALF)]

    def up(k, c):
        ref = chunk_of((z + NZ - k) % NZ, c)
        return remote(ref, ref, zus.at[4 * k + c], zur.at[4 * k + c], z_up, b)

    def down(k, c):
        ref = chunk_of((z + k) % NZ, c)
        return remote(ref, ref, zds.at[4 * k + c], zdr.at[4 * k + c], z_down, b)

    def from_below(k, c):
        ref = chunk_of((z + NZ - 1 - k) % NZ, c)
        remote(ref, ref, zus.at[4 * k + c], zur.at[4 * k + c], z_up, b).wait_recv()

    def from_above(k, c):
        ref = chunk_of((z + 1 + k) % NZ, c)
        remote(ref, ref, zds.at[4 * k + c], zdr.at[4 * k + c], z_down, b).wait_recv()

    def halo_up(k):
        zz = (z + NZ - k) % NZ
        ref = hq.at[zz] if k < 3 else hq.at[zz, 0]
        return remote(ref, ref, zhus.at[k], zhur.at[k], z_up, b)

    def halo_down(k):
        zz = (z + k) % NZ
        ref = hq.at[zz] if k < 3 else hq.at[zz, 1]
        return remote(ref, ref, zhds.at[k], zhdr.at[k], z_down, b)

    def halo_below(k):
        zz = (z + NZ - 1 - k) % NZ
        ref = hq.at[zz] if k < 3 else hq.at[zz, 0]
        remote(ref, ref, zhus.at[k], zhur.at[k], z_up, b).wait_recv()

    def halo_above(k):
        zz = (z + 1 + k) % NZ
        ref = hq.at[zz] if k < 3 else hq.at[zz, 1]
        remote(ref, ref, zhds.at[k], zhdr.at[k], z_down, b).wait_recv()

    def x_arrived(d):
        ref = pbuf.at[(x + NX - d) % NX]
        remote(ref, ref, xs.at[d - 1], xr.at[d - 1], z_up, b).wait_recv()

    @pl.when(home)
    def _():
        for c in range(2):
            up(0, c).start()
            down(0, c).start()

    remote(hp.at[x], hp.at[x], hs.at[0], hr.at[0], a, b_prev).wait_recv()
    for d in range(1, 4):
        go(remote(
            hp.at[x], hp.at[x], xhs.at[d - 1], xhr.at[d - 1], tap_of(y_hi, (x + d) % NX, z), b
        ))
    go(remote(hp.at[x], hq.at[z, x % 2], chs.at[0], chr_.at[x % 2], far_tap, b))
    x_arrived(3)

    @pl.when(home)
    def _():
        qbuf[z, 1] = pbuf[x + 1]
        for c in range(2, 4):
            up(0, c).start()
            down(0, c).start()

    @pl.when(away)
    def _():
        for c in range(4):
            ref = chunk_of(z, c)
            remote(ref, ref, cs.at[0], cr.at[c], far_tap, b).wait_recv()
            up(0, c).start()
            down(0, c).start()

    for c in range(4):
        sends.append(up(0, c))
        sends.append(down(0, c))
    x_arrived(1)
    x_arrived(2)
    for d in range(1, 4):
        ref = hp.at[(x + NX - d) % NX]
        remote(ref, ref, xhs.at[d - 1], xhr.at[d - 1], z_up, b).wait_recv()

    @pl.when(home)
    def _():
        hq[z, 0] = hp[x]
        hq[z, 1] = hp[x + 1]

    @pl.when(away)
    def _():
        for s in range(2):
            ref = hq.at[z, s]
            remote(ref, ref, chs.at[0], chr_.at[s], far_tap, b).wait_recv()

    go(halo_up(0))
    go(halo_down(0))

    val = details_of(
        jnp.concatenate([pbuf[i] for i in range(NX)], axis=0),
        jnp.concatenate([hp[i] for i in range(NX)], axis=0),
        wbuf,
    )
    for w in range(NWIN):
        for j in range(LEVELS):
            dp[j, :, w * OUT : (w + 1) * OUT] = val[
                w * NX * ROWS : (w + 1) * NX * ROWS, j * OUT : (j + 1) * OUT
            ]

    def columns(m):
        zz = (z + m) % NZ
        k, h = PIECE[m]
        val = details_of(
            jnp.concatenate([qbuf[zz, 0], qbuf[zz, 1]], axis=0),
            jnp.concatenate([hq[zz, 0], hq[zz, 1]], axis=0),
            wbuf,
        )
        for w in range(NWIN):
            for s in range(2):
                first = (2 * w + s) * ROWS
                to = s * 64 + h * ROWS
                for j in range(LEVELS):
                    dq[k, j, to : to + ROWS, w * OUT : (w + 1) * OUT] = (
                        val[first : first + ROWS, j * OUT : (j + 1) * OUT]
                    )

    def product(k):
        for j in range(LEVELS):
            prod = lax.dot_general(dp[j], dq[k, j], NT, preferred_element_type=jnp.float32)
            part[k, 0, j] = prod[0:64]
            part[k, 1, j] = prod[64:128]
        go(remote(part.at[k, 1 - core], sib.at[k], ss.at[k], sr.at[k], a, sibling))

    def x_copy(k, i):
        there = 2 * core + i
        d = (there - x + NX) % NX
        return remote(
            red.at[k, i], xo.at[k, x], xos.at[2 * k + i], xor_.at[3 * k + d - 1],
            tap_of(y_hi, there, z), b,
        )

    def x_out(k):
        ref = sib.at[k]
        remote(ref, ref, ss.at[k], sr.at[k], a, sibling).wait_recv()
        for i in range(2):
            red[k, i] = part[k, core, :, i * ROWS : (i + 1) * ROWS] + sib[k, :, i * ROWS : (i + 1) * ROWS]
            pl.when(2 * core + i != x)(lambda: x_copy(k, i).start())

        @pl.when(post)
        def _():
            xo[k, x] = red[k, x % 2]

    def x_for(t):
        return 2 * (t % 2) + jnp.where(t // 2 == y_hi, 0, 1)

    def y_copy(k, d):
        there = (y_lo + d) % NYL
        return remote(
            xo.at[k, x_for(there)], yo.at[k, d - 1], yos.at[3 * k + d - 1], yor.at[3 * k + d - 1],
            a, there * 2 + core,
        )

    def y_out(k):
        @pl.when(post)
        def _():
            for d in range(1, 4):
                ref = xo.at[k, (x + NX - d) % NX]
                remote(ref, ref, xos.at[0], xor_.at[3 * k + d - 1], z_up, b).wait_recv()
            for d in range(1, 4):
                y_copy(k, d).start()

    def fin_copy(k):
        return remote(fin.at[k], fin.at[k], fs.at[k], fr.at[k], a, sibling)

    def finish(k):
        @pl.when(post)
        def _():
            for d in range(1, 4):
                ref = yo.at[k, d - 1]
                remote(ref, ref, yos.at[0], yor.at[3 * k + d - 1], a, sibling).wait_recv()
            total = xo[k, x_for(y_lo)] + yo[k, 0] + yo[k, 1] + yo[k, 2]
            fin[k] = total * (1.0 / (WIDTH * 8))
            fin_copy(k).start()

    columns(0)
    for k in range(3):
        for c in range(4):
            from_below(k, c)
            if k < 2 or c < 2:
                go(up(k + 1, c))
            from_above(k, c)
            if k < 2 or c >= 2:
                go(down(k + 1, c))
            if c == 1 and k >= 1:
                x_out(k - 1)
        halo_below(k)
        go(halo_up(k + 1))
        halo_above(k)
        go(halo_down(k + 1))
        columns(1 + k)
        columns(7 - k)
        product(k)
        if k >= 2:
            y_out(k - 2)
    from_below(3, 0)
    from_above(3, 2)
    x_out(2)
    y_out(1)
    from_below(3, 1)
    from_above(3, 3)
    halo_below(3)
    halo_above(3)
    columns(4)
    product(3)
    x_out(3)
    y_out(2)
    finish(0)
    finish(1)
    y_out(3)
    finish(2)
    finish(3)

    @pl.when(jnp.logical_not(post))
    def _():
        for k in range(CHUNKS):
            fin_copy(k).wait_recv()

    group = lax.broadcasted_iota(jnp.int32, (ROWS, 128), 1) // ROWS
    for j in range(LEVELS):
        mine = []
        for k in range(CHUNKS):
            v = fin[k, j]
            mine.append(jnp.where(core == 0, v, pltpu.roll(v, 64, 1)))
        low = mine[3]
        high = pltpu.roll(mine[3], 96, 1)
        for k in range(3):
            low = jnp.where(group == k + 1, pltpu.roll(mine[k], 32 * (k + 1), 1), low)
            moved = mine[k] if k == 2 else pltpu.roll(mine[k], 64 - 32 * k, 1)
            high = jnp.where(group == 3 - k, moved, high)
        o_ref[j] = pltpu.roll(jnp.concatenate([low, high], axis=1), z * ROWS, 1)

    for copy in sends:
        copy.wait_send()
    for k in range(CHUNKS):
        for i in range(2):
            pl.when(2 * core + i != x)(lambda: x_copy(k, i).wait_send())

    @pl.when(post)
    def _():
        for k in range(CHUNKS):
            for d in range(1, 4):
                y_copy(k, d).wait_send()
            fin_copy(k).wait_send()


def body(pressure, filters):
    def sems(*counts):
        return [pltpu.SemaphoreType.DMA((n,)) for n in counts for _ in range(2)]

    f32, bf16 = jnp.float32, jnp.bfloat16
    return pl.pallas_call(
        kernel,
        out_shape=jax.ShapeDtypeStruct((LEVELS, ROWS, 256), f32),
        in_specs=[
            pl.BlockSpec(memory_space=pltpu.VMEM),
            pl.BlockSpec(memory_space=pltpu.SMEM),
        ],
        out_specs=pl.BlockSpec(memory_space=pltpu.VMEM),
        scratch_shapes=[
            pltpu.VMEM((NX, ROWS, WIDTH), bf16),
            pltpu.VMEM((NX, ROWS, HALO), bf16),
            pltpu.VMEM((NZ, 2, ROWS, WIDTH), bf16),
            pltpu.VMEM((NZ, 2, ROWS, HALO), bf16),
            pltpu.VMEM((SPLITS, WIN, LEVELS * OUT), bf16),
            pltpu.VMEM((LEVELS, NX * ROWS, WIDTH), bf16),
            pltpu.VMEM((CHUNKS, LEVELS, 128, WIDTH), bf16),
            pltpu.VMEM((CHUNKS, 2, LEVELS, 64, 128), f32),
            pltpu.VMEM((CHUNKS, LEVELS, 64, 128), f32),
            pltpu.VMEM((CHUNKS, 2, LEVELS, ROWS, 128), f32),
            pltpu.VMEM((CHUNKS, NX, LEVELS, ROWS, 128), f32),
            pltpu.VMEM((CHUNKS, 3, LEVELS, ROWS, 128), f32),
            pltpu.VMEM((CHUNKS, LEVELS, ROWS, 128), f32),
            *sems(1, 3, 3, 4, 2, 16, 16, 4, 4, CHUNKS, 3 * CHUNKS, 3 * CHUNKS, CHUNKS),
        ],
        compiler_params=pltpu.CompilerParams(
            collective_id=0, has_side_effects=True, vmem_limit_bytes=40 * 1024 * 1024
        ),
        cost_estimate=pl.CostEstimate(
            flops=4_000_000_000, bytes_accessed=200_000, transcendentals=0
        ),
    )(pressure, filters)


def solution(mesh):
    placed = (P("tap", "tm"), P())
    return jax.shard_map(
        body, mesh=mesh, in_specs=placed, out_specs=P(None, "tap", "tm"), check_vma=False
    )
```

time: 62.4 us -> 52.7 us (0.84)
  the two profiles are of different devices: /device:TPU:8 before, /device:TPU:1 now
where the time goes in v2:
time: 52.7 us; the launch traced here: 52.5 us
  Pallas kernels  50.3 us (95%)
  local copies, waits for them, and re-layouts  2.16 us (4%)
    pallas_call x1, Pallas kernels, body(): pl.pallas_call(kernel, out_shape=jax.ShapeDtypeStruct((LEVELS, ROWS, 256)...  50.3 us
    unnamed x5, local copies, waits for them, and re-layouts  2.16 us

profile of v2, /device:TPU:1, one launch (start us, length us, event | category | flops | bytes accessed | tf_op | source)
XLA Modules:
  0.0 52.5 jit_solution(13786577239478335167)
XLA Ops:
  0.0 0.0 copy-start
  0.0 0.8 %copy-done = bf16[32,1024]{1,0:T(8,128)(2,1)S(1)} copy-done((bf16[32,1024]{1,0:T(8,128)(2,1)S(1)}, bf16[32,1024]{1,0:T(8,128)(2,1)}, u32[]{:S(2)}) %copy-start) | copy-done | bytes 65560
  0.8 0.0 copy-start.1
  0.8 0.7 %copy-done.1 = f32[2,16]{1,0:T(2,128)S(1)} copy-done((f32[2,16]{1,0:T(2,128)S(1)}, f32[2,16]{1,0:T(2,128)}, u32[]{:S(2)}) %copy-start.1) | copy-done | bytes 152
  1.5 50.3 %shard_map.28 = f32[3,32,256]{2,1,0:T(8,128)S(1)} custom-call(bf16[32,1024]{1,0:T(8,128)(2,1)S(1)} %copy-done, f32[2,16]{1,0:T(2,128)S(1)} %copy-done.1), custom_call_target="tpu_custom_call" | custom-call | flops 4000000000 | bytes 200000 | tf_op jit(solution)/shard_map/pallas_call | solution.py:404
  51.9 0.6 %copy.4 = f32[3,32,256]{2,1,0:T(8,128)} copy(f32[3,32,256]{2,1,0:T(8,128)S(1)} %shard_map.28) | data formatting | bytes 196608
Async XLA Ops:
  0.0 0.8 %copy-start = (bf16[32,1024]{1,0:T(8,128)(2,1)S(1)}, bf16[32,1024]{1,0:T(8,128)(2,1)}, u32[]{:S(2)}) copy-start(bf16[32,1024]{1,0:T(8,128)(2,1)} %p_ref.1) | copy-start | bytes 196612
  0.8 0.7 %copy-start.1 = (f32[2,16]{1,0:T(2,128)S(1)}, f32[2,16]{1,0:T(2,128)}, u32[]{:S(2)}) copy-start(f32[2,16]{1,0:T(2,128)} %f_ref.1) | copy-start | bytes 388

commit v3 on v0

v3 whole, which is shorter than its diff:
```python
import jax
import jax.numpy as jnp
from jax import lax
from jax.experimental import pallas as pl
from jax.experimental.pallas import tpu as pltpu
from jax.sharding import PartitionSpec as P

FILT = 16
LEVELS = 3
NX, NZ, NYL = 4, 8, 4
ROWS = 32
WIDTH = 1024
HALO = 128
WIN = 256
OUT = 128
NWIN = WIDTH // OUT
SPLITS = 3
LANES = 384
CHUNKS = 4
HALF = 16
MESH = pl.DeviceIdType.MESH
NT = (((1,), (1,)), ((), ()))


def remote(src, dst, send, recv, tap, tm):
    return pltpu.make_async_remote_copy(
        src_ref=src, dst_ref=dst, send_sem=send, recv_sem=recv,
        device_id=(tap, tm), device_id_type=MESH,
    )


def build_bands(f_ref, wbuf):
    lane = lax.broadcasted_iota(jnp.int32, (8, LANES), 1)

    def comb(row, top, step):
        line = jnp.zeros((8, LANES), jnp.float32)
        for k in range(FILT):
            line = jnp.where(lane == top - step * k, f_ref[row, k], line)
        return line

    def smoothed(line, step):
        total = jnp.zeros((8, LANES), jnp.float32)
        for k in range(FILT):
            moved = line if k == 0 else pltpu.roll(line, LANES - step * k, 1)
            total = total + f_ref[1, k] * moved
        return total

    lines = [
        comb(0, 328, 1),
        smoothed(comb(0, 344, 2), 1),
        smoothed(smoothed(comb(0, 376, 4), 2), 1),
    ]
    for level, line in enumerate(lines):
        wide = jnp.broadcast_to(line[0:1, :], (WIN, LANES))
        band = pltpu.roll(wide, 0, 1, stride=1, stride_axis=0)[:, :OUT]
        for piece in range(SPLITS):
            part = band.astype(jnp.bfloat16)
            wbuf[piece, :, level * OUT : (level + 1) * OUT] = part
            band = band - part.astype(jnp.float32)


def details_of(main, halo, wbuf):
    ext = jnp.concatenate([main, halo], axis=1)
    windows = jnp.concatenate([ext[:, w * OUT : w * OUT + WIN] for w in range(NWIN)], axis=0)
    total = jnp.dot(windows, wbuf[0], preferred_element_type=jnp.float32)
    for piece in range(1, SPLITS):
        total += jnp.dot(windows, wbuf[piece], preferred_element_type=jnp.float32)
    return total.astype(jnp.bfloat16)


def kernel(
    p_ref, f_ref, o_ref,
    pbuf, hp, qbuf, hq, wbuf, dp, dq, part, sib, red, xo, yo,
    ps, hs, hr, xs, xr, xhs, xhr, cs, cr, chs, chr_, zus, zur, zds, zdr, zhs, zhr,
    ss, sr, xos, xor_, yos, yor,
):
    a = lax.axis_index("tap")
    b = lax.axis_index("tm")
    y_hi = a // (NX * NZ)
    x = (a // NZ) % NX
    z = a % NZ
    y_lo = b // 2
    core = b % 2

    def tap_of(yh, xx, zz):
        return yh * (NX * NZ) + xx * NZ + zz

    b_next = (b + 1) % 8
    b_prev = (b + 7) % 8
    post = x % 2 == core
    far_tap = tap_of(1 - y_hi, x, z)
    z_up = tap_of(y_hi, x, (z + 1) % NZ)
    z_down = tap_of(y_hi, x, (z + NZ - 1) % NZ)
    sibling = y_lo * 2 + (1 - core)

    fetch = pltpu.make_async_copy(p_ref, pbuf.at[x], ps.at[0])
    fetch.start()
    barrier = pltpu.get_barrier_semaphore()

    def hello(tap, tm):
        pl.semaphore_signal(barrier, inc=1, device_id=(tap, tm), device_id_type=MESH)

    for d in (1, 7, 2, 6, 3, 5, 4):
        hello(tap_of(y_hi, x, (z + d) % NZ), b)
    hello(far_tap, b)
    hello(a, b_next)
    hello(a, b_prev)
    for d in range(1, 4):
        hello(a, (b + 2 * d) % 8)
        hello(tap_of(y_hi, (x + d) % NX, z), b)

    build_bands(f_ref, wbuf)
    fetch.wait()
    pl.semaphore_wait(barrier, 16)

    sends = []

    def go(copy):
        copy.start()
        sends.append(copy)

    def rows_of(c):
        return pl.ds(c * HALF, HALF)

    def up(t, k, c):
        dst = qbuf.at[t, (z + NZ - k) % NZ, rows_of(c)]
        src = pbuf.at[x, rows_of(c)] if t == 0 and k == 0 else dst
        n = 8 * t + 2 * k + c
        return remote(src, dst, zus.at[n], zur.at[n], z_up, b)

    def down(t, k, c):
        dst = qbuf.at[t, (z + k) % NZ, rows_of(c)]
        src = pbuf.at[x, rows_of(c)] if t == 0 and k == 0 else dst
        n = 8 * t + 2 * k + c
        return remote(src, dst, zds.at[n], zdr.at[n], z_down, b)

    def from_below(t, k, c):
        ref = qbuf.at[t, (z + NZ - 1 - k) % NZ, rows_of(c)]
        n = 8 * t + 2 * k + c
        remote(ref, ref, zus.at[n], zur.at[n], z_up, b).wait_recv()

    def from_above(t, k, c):
        ref = qbuf.at[t, (z + 1 + k) % NZ, rows_of(c)]
        n = 8 * t + 2 * k + c
        remote(ref, ref, zds.at[n], zdr.at[n], z_down, b).wait_recv()

    def far(m, c):
        zz = (z + m) % NZ
        src = pbuf.at[x, rows_of(c)] if m == 0 else qbuf.at[0, zz, rows_of(c)]
        n = (2 if m else 0) + c
        return remote(src, qbuf.at[1, zz, rows_of(c)], cs.at[n], cr.at[n], far_tap, b)

    def from_far(m, c):
        ref = qbuf.at[1, (z + m) % NZ, rows_of(c)]
        n = (2 if m else 0) + c
        remote(ref, ref, cs.at[n], cr.at[n], far_tap, b).wait_recv()

    def send_halos(t):
        src = hp.at[x] if t == 0 else hq.at[1, z]
        for d in (1, 7, 2, 6, 3, 5, 4):
            n = 7 * t + d - 1
            go(remote(
                src, hq.at[t, z], zhs.at[n], zhr.at[n], tap_of(y_hi, x, (z + d) % NZ), b
            ))

    def halo_from(t, m):
        ref = hq.at[t, (z + m) % NZ]
        n = 7 * t + (NZ - m) - 1
        remote(ref, ref, zhs.at[n], zhr.at[n], z_up, b).wait_recv()

    def step(t, k):
        for c in range(2):
            from_below(t, k, c)
            if k < 2 or (t == 0 and c == 0):
                go(up(t, k + 1, c))
            from_above(t, k, c)
            if k < 2 or (t == 0 and c == 1):
                go(down(t, k + 1, c))

    def columns(t, *places):
        for m in places:
            if m:
                halo_from(t, m)
        val = details_of(
            jnp.concatenate([qbuf[t, (z + m) % NZ] for m in places], axis=0),
            jnp.concatenate([hq[t, (z + m) % NZ] for m in places], axis=0),
            wbuf,
        )
        for w in range(NWIN):
            for n, m in enumerate(places):
                first = (len(places) * w + n) * ROWS
                q, to = 2 * t + (m + 1) % NZ // 4, (m + 1) % 4 * ROWS
                for j in range(LEVELS):
                    dq[q, j, to : to + ROWS, w * OUT : (w + 1) * OUT] = (
                        val[first : first + ROWS, j * OUT : (j + 1) * OUT]
                    )

    def sib_copy(q):
        return remote(part.at[q], sib.at[q], ss.at[q], sr.at[q], a, sibling)

    def product(q):
        for j in range(LEVELS):
            part[q, j] = lax.dot_general(dp[j], dq[q, j], NT, preferred_element_type=jnp.float32)
        pl.when(jnp.logical_not(post))(lambda: sib_copy(q).start())

    def x_copy(q, d):
        there = (x + d) % NX
        return remote(
            red.at[q, there], xo.at[q, x // 2], xos.at[3 * q + d - 1], xor_.at[2 * q + x // 2],
            tap_of(y_hi, there, z), b,
        )

    def x_out(q):
        @pl.when(post)
        def _():
            sib_copy(q).wait_recv()
            for i in range(NX):
                rows = slice(i * ROWS, (i + 1) * ROWS)
                red[q, i] = part[q, :, rows] + sib[q, :, rows]
            for d in (2, 1, 3):
                x_copy(q, d).start()
            xo[q, x // 2] = red[q, x]

    def y_goal(q, i):
        return 2 * (y_hi if q < 2 else 1 - y_hi) + i

    def y_copy(q, i):
        goal = y_goal(q, i)
        d = (goal - y_lo + NYL) % NYL
        n = 3 * (q % 2) + d - 1
        return remote(
            xo.at[q, i], yo.at[q % 2, d - 1], yos.at[2 * q + i], yor.at[n], a, goal * 2 + core
        )

    def y_out(q):
        for i in range(2):
            @pl.when(2 * i + core != x)
            def _():
                ref = xo.at[q, i]
                remote(ref, ref, xos.at[0], xor_.at[2 * q + i], z_up, b).wait_recv()

            pl.when(y_goal(q, i) != y_lo)(lambda: y_copy(q, i).start())

    for c in range(2):
        go(far(0, c))
    go(remote(pbuf.at[x, :, pl.ds(0, HALO)], hp.at[x], hs.at[0], hr.at[0], a, b_prev))
    for c in range(2):
        go(up(0, 0, c))
        go(down(0, 0, c))
    for d in range(1, 4):
        go(remote(
            pbuf.at[x], pbuf.at[x], xs.at[d - 1], xr.at[d - 1], tap_of(y_hi, (x + d) % NX, z), b
        ))

    step(0, 0)
    remote(hp.at[x], hp.at[x], hs.at[0], hr.at[0], a, b_prev).wait_recv()
    go(remote(hp.at[x], hq.at[1, z], chs.at[0], chr_.at[0], far_tap, b))
    for d in range(1, 4):
        go(remote(
            hp.at[x], hp.at[x], xhs.at[d - 1], xhr.at[d - 1], tap_of(y_hi, (x + d) % NX, z), b
        ))
    send_halos(0)
    for d in range(1, 4):
        ref = pbuf.at[(x + NX - d) % NX]
        remote(ref, ref, xs.at[d - 1], xr.at[d - 1], z_up, b).wait_recv()
    step(0, 1)
    for c in range(2):
        from_far(0, c)
        go(up(1, 0, c))
        go(down(1, 0, c))
    for d in range(1, 4):
        ref = hp.at[(x + NX - d) % NX]
        remote(ref, ref, xhs.at[d - 1], xhr.at[d - 1], z_up, b).wait_recv()
    val = details_of(
        jnp.concatenate([pbuf[i] for i in range(NX)], axis=0),
        jnp.concatenate([hp[i] for i in range(NX)], axis=0),
        wbuf,
    )
    for w in range(NWIN):
        for j in range(LEVELS):
            dp[j, :, w * OUT : (w + 1) * OUT] = val[
                w * NX * ROWS : (w + 1) * NX * ROWS, j * OUT : (j + 1) * OUT
            ]
    own = pl.ds(pl.multiple_of(x * ROWS, ROWS), ROWS)
    for j in range(LEVELS):
        dq[0, j, ROWS : 2 * ROWS] = dp[j, own, :]
    remote(hq.at[1, z], hq.at[1, z], chs.at[0], chr_.at[0], far_tap, b).wait_recv()
    send_halos(1)
    columns(0, 1, 7)
    step(0, 2)
    columns(0, 2, 6)
    product(0)
    step(1, 0)
    from_below(0, 3, 0)
    go(far(4, 0))
    from_above(0, 3, 1)
    go(far(4, 1))
    x_out(0)
    columns(0, 3, 5)
    columns(0, 4)
    product(1)
    step(1, 1)
    columns(1, 0, 1)
    columns(1, 7, 2)
    product(2)
    x_out(1)
    y_out(0)
    columns(1, 6)
    x_out(2)
    step(1, 2)
    columns(1, 3, 5)
    y_out(1)
    for c in range(2):
        from_far(4, c)
    columns(1, 4)
    product(3)
    y_out(2)
    x_out(3)
    y_out(3)

    kind = jnp.where(y_lo // 2 == y_hi, 0, 2)
    totals = []
    for h in range(2):
        for d in range(1, 4):
            ref = yo.at[h, d - 1]
            remote(ref, ref, yos.at[0], yor.at[3 * h + d - 1], a, sibling).wait_recv()
        totals.append(xo[kind + h, y_lo % 2] + yo[h, 0] + yo[h, 1] + yo[h, 2])
    total = jnp.concatenate(totals, axis=2) * (1.0 / (WIDTH * 8))
    for j in range(LEVELS):
        o_ref[j] = pltpu.roll(total[j], ((z + NZ - 1) % NZ) * ROWS, 1)

    for copy in sends:
        copy.wait_send()
    for q in range(CHUNKS):
        @pl.when(post)
        def _():
            for d in range(1, 4):
                x_copy(q, d).wait_send()

        pl.when(jnp.logical_not(post))(lambda: sib_copy(q).wait_send())
        for i in range(2):
            pl.when(y_goal(q, i) != y_lo)(lambda: y_copy(q, i).wait_send())


def body(pressure, filters):
    def sems(*counts):
        return [pltpu.SemaphoreType.DMA((n,)) for n in counts for _ in range(2)]

    f32, bf16 = jnp.float32, jnp.bfloat16
    return pl.pallas_call(
        kernel,
        out_shape=jax.ShapeDtypeStruct((LEVELS, ROWS, 256), f32),
        in_specs=[
            pl.BlockSpec(memory_space=pltpu.HBM),
            pl.BlockSpec(memory_space=pltpu.SMEM),
        ],
        out_specs=pl.BlockSpec(memory_space=pltpu.VMEM),
        scratch_shapes=[
            pltpu.VMEM((NX, ROWS, WIDTH), bf16),
            pltpu.VMEM((NX, ROWS, HALO), bf16),
            pltpu.VMEM((2, NZ, ROWS, WIDTH), bf16),
            pltpu.VMEM((2, NZ, ROWS, HALO), bf16),
            pltpu.VMEM((SPLITS, WIN, LEVELS * OUT), bf16),
            pltpu.VMEM((LEVELS, NX * ROWS, WIDTH), bf16),
            pltpu.VMEM((CHUNKS, LEVELS, 128, WIDTH), bf16),
            pltpu.VMEM((CHUNKS, LEVELS, NX * ROWS, 128), f32),
            pltpu.VMEM((CHUNKS, LEVELS, NX * ROWS, 128), f32),
            pltpu.VMEM((CHUNKS, NX, LEVELS, ROWS, 128), f32),
            pltpu.VMEM((CHUNKS, 2, LEVELS, ROWS, 128), f32),
            pltpu.VMEM((2, 3, LEVELS, ROWS, 128), f32),
            pltpu.SemaphoreType.DMA((1,)),
            *sems(1, 3, 3, 4, 1, 16, 16, 14, CHUNKS, 3 * CHUNKS, 2 * CHUNKS),
        ],
        compiler_params=pltpu.CompilerParams(
            collective_id=0, has_side_effects=True, vmem_limit_bytes=40 * 1024 * 1024
        ),
        cost_estimate=pl.CostEstimate(
            flops=4_000_000_000, bytes_accessed=200_000, transcendentals=0
        ),
    )(pressure, filters)


def solution(mesh):
    placed = (P("tap", "tm"), P())
    return jax.shard_map(
        body, mesh=mesh, in_specs=placed, out_specs=P(None, "tap", "tm"), check_vma=False
    )
```

time: 377 us -> 50.1 us (0.13)
  the two profiles are of different devices: /device:TPU:2 before, /device:TPU:25 now
where the time goes in v3:
time: 50.1 us; the launch traced here: 49.9 us
  Pallas kernels  47.8 us (95%)
  local copies, waits for them, and re-layouts  2.16 us (4%)
    pallas_call x1, Pallas kernels, body(): pl.pallas_call(kernel, out_shape=jax.ShapeDtypeStruct((LEVELS, ROWS, 256)...  47.8 us
    unnamed x5, local copies, waits for them, and re-layouts  2.16 us

profile of v3, /device:TPU:25, one launch (start us, length us, event | category | flops | bytes accessed | tf_op | source)
XLA Modules:
  0.0 49.9 jit_solution(1165828805039310564)
XLA Ops:
  0.0 0.0 copy-start
  0.0 0.8 %copy-done = bf16[32,1024]{1,0:T(8,128)(2,1)S(1)} copy-done((bf16[32,1024]{1,0:T(8,128)(2,1)S(1)}, bf16[32,1024]{1,0:T(8,128)(2,1)}, u32[]{:S(2)}) %copy-start) | copy-done | bytes 65560
  0.8 0.0 copy-start.1
  0.8 0.7 %copy-done.1 = f32[2,16]{1,0:T(2,128)S(1)} copy-done((f32[2,16]{1,0:T(2,128)S(1)}, f32[2,16]{1,0:T(2,128)}, u32[]{:S(2)}) %copy-start.1) | copy-done | bytes 152
  1.5 47.8 %shard_map.28 = f32[3,32,256]{2,1,0:T(8,128)S(1)} custom-call(bf16[32,1024]{1,0:T(8,128)(2,1)S(1)} %copy-done, f32[2,16]{1,0:T(2,128)S(1)} %copy-done.1), custom_call_target="tpu_custom_call" | custom-call | flops 4000000000 | bytes 200000 | tf_op jit(solution)/shard_map/pallas_call | solution.py:350
  49.3 0.6 %copy.4 = f32[3,32,256]{2,1,0:T(8,128)} copy(f32[3,32,256]{2,1,0:T(8,128)S(1)} %shard_map.28) | data formatting | bytes 196608
Async XLA Ops:
  0.0 0.8 %copy-start = (bf16[32,1024]{1,0:T(8,128)(2,1)S(1)}, bf16[32,1024]{1,0:T(8,128)(2,1)}, u32[]{:S(2)}) copy-start(bf16[32,1024]{1,0:T(8,128)(2,1)} %p_ref.1) | copy-start | bytes 196612
  0.8 0.7 %copy-start.1 = (f32[2,16]{1,0:T(2,128)S(1)}, f32[2,16]{1,0:T(2,128)}, u32[]{:S(2)}) copy-start(f32[2,16]{1,0:T(2,128)} %f_ref.1) | copy-start | bytes 388

commit v4 on v3

--- a/solution.py
+++ b/solution.py
@@ -18,6 +18,7 @@
 LANES = 384
 CHUNKS = 4
 HALF = 16
+HOPS = ((0, 2, 0), (0, 2, 1), (0, 1, 2), (2, 1, 0), (2, 1, 1), (2, 2, None))
 MESH = pl.DeviceIdType.MESH
 NT = (((1,), (1,)), ((), ()))
 
@@ -71,7 +72,7 @@
 def kernel(
     p_ref, f_ref, o_ref,
     pbuf, hp, qbuf, hq, wbuf, dp, dq, part, sib, red, xo, yo,
-    ps, hs, hr, xs, xr, xhs, xhr, cs, cr, chs, chr_, zus, zur, zds, zdr, zhs, zhr,
+    ps, hs, hr, xs, xr, xhs, xhr, cs, cr, chs, chr_, zs, zr, zhs, zhr, ths, thr,
     ss, sr, xos, xor_, yos, yor,
 ):
     a = lax.axis_index("tap")
@@ -90,7 +91,6 @@
     post = x % 2 == core
     far_tap = tap_of(1 - y_hi, x, z)
     z_up = tap_of(y_hi, x, (z + 1) % NZ)
-    z_down = tap_of(y_hi, x, (z + NZ - 1) % NZ)
     sibling = y_lo * 2 + (1 - core)
 
     fetch = pltpu.make_async_copy(p_ref, pbuf.at[x], ps.at[0])
@@ -122,27 +122,48 @@
     def rows_of(c):
         return pl.ds(c * HALF, HALF)
 
-    def up(t, k, c):
-        dst = qbuf.at[t, (z + NZ - k) % NZ, rows_of(c)]
-        src = pbuf.at[x, rows_of(c)] if t == 0 and k == 0 else dst
-        n = 8 * t + 2 * k + c
-        return remote(src, dst, zus.at[n], zur.at[n], z_up, b)
-
-    def down(t, k, c):
-        dst = qbuf.at[t, (z + k) % NZ, rows_of(c)]
-        src = pbuf.at[x, rows_of(c)] if t == 0 and k == 0 else dst
-        n = 8 * t + 2 * k + c
-        return remote(src, dst, zds.at[n], zdr.at[n], z_down, b)
-
-    def from_below(t, k, c):
-        ref = qbuf.at[t, (z + NZ - 1 - k) % NZ, rows_of(c)]
-        n = 8 * t + 2 * k + c
-        remote(ref, ref, zus.at[n], zur.at[n], z_up, b).wait_recv()
-
-    def from_above(t, k, c):
-        ref = qbuf.at[t, (z + 1 + k) % NZ, rows_of(c)]
-        n = 8 * t + 2 * k + c
-        remote(ref, ref, zds.at[n], zdr.at[n], z_down, b).wait_recv()
+    def hop(t, way, n):
+        behind, dist, rows = HOPS[n]
+        if rows is None:
+            rows = 0 if way == 1 else 1
+        span = pl.ds(0, ROWS) if rows == 2 else rows_of(rows)
+        slot = (z + NZ - way * behind) % NZ
+        dst = qbuf.at[t, slot, span]
+        src = pbuf.at[x, span] if t == 0 and behind == 0 else dst
+        i = (6 * t + n) * 2 + (way + 1) // 2
+        return remote(
+            src, dst, zs.at[i], zr.at[i], tap_of(y_hi, x, (z + NZ + way * dist) % NZ), b
+        )
+
+    def arrived(t, way, n):
+        behind, dist, rows = HOPS[n]
+        if rows is None:
+            rows = 0 if way == 1 else 1
+        span = pl.ds(0, ROWS) if rows == 2 else rows_of(rows)
+        ref = qbuf.at[t, (z + NZ - way * (behind + dist)) % NZ, span]
+        i = (6 * t + n) * 2 + (way + 1) // 2
+        remote(ref, ref, zs.at[i], zr.at[i], z_up, b).wait_recv()
+
+    def first_hops(t, *ns):
+        for n in ns:
+            for way in (1, -1):
+                go(hop(t, way, n))
+
+    def pass_on(t):
+        for c in range(2):
+            for way in (1, -1):
+                arrived(t, way, c)
+                if t == 0 and c == (1 - way) // 2:
+                    go(hop(t, way, 5))
+                go(hop(t, way, 3 + c))
+        if t == 0:
+            go(later_halo(6))
+            go(later_halo(2))
+
+    def wait_for(t, *ns):
+        for n in ns:
+            for way in (1, -1):
+                arrived(t, way, n)
 
     def far(m, c):
         zz = (z + m) % NZ
@@ -155,27 +176,25 @@
         n = (2 if m else 0) + c
         remote(ref, ref, cs.at[n], cr.at[n], far_tap, b).wait_recv()
 
-    def send_halos(t):
-        src = hp.at[x] if t == 0 else hq.at[1, z]
-        for d in (1, 7, 2, 6, 3, 5, 4):
-            n = 7 * t + d - 1
-            go(remote(
-                src, hq.at[t, z], zhs.at[n], zhr.at[n], tap_of(y_hi, x, (z + d) % NZ), b
-            ))
+    def owner_halo(m):
+        d = NZ - m
+        return remote(
+            hq.at[1, z], hq.at[1, z], zhs.at[d - 1], zhr.at[d - 1],
+            tap_of(y_hi, x, (z + d) % NZ), b,
+        )
+
+    def later_halo(m):
+        zz = (z + m) % NZ
+        return remote(
+            qbuf.at[0, zz, :, pl.ds(0, HALO)], hq.at[0, zz], ths.at[m], thr.at[m], a, b_prev
+        )
 
     def halo_from(t, m):
-        ref = hq.at[t, (z + m) % NZ]
-        n = 7 * t + (NZ - m) - 1
-        remote(ref, ref, zhs.at[n], zhr.at[n], z_up, b).wait_recv()
-
-    def step(t, k):
-        for c in range(2):
-            from_below(t, k, c)
-            if k < 2 or (t == 0 and c == 0):
-                go(up(t, k + 1, c))
-            from_above(t, k, c)
-            if k < 2 or (t == 0 and c == 1):
-                go(down(t, k + 1, c))
+        if t == 1:
+            ref = hq.at[1, (z + m) % NZ]
+            remote(ref, ref, zhs.at[NZ - m - 1], zhr.at[NZ - m - 1], z_up, b).wait_recv()
+        else:
+            later_halo(m).wait_recv()
 
     def columns(t, *places):
         for m in places:
@@ -244,30 +263,30 @@
     for c in range(2):
         go(far(0, c))
     go(remote(pbuf.at[x, :, pl.ds(0, HALO)], hp.at[x], hs.at[0], hr.at[0], a, b_prev))
-    for c in range(2):
-        go(up(0, 0, c))
-        go(down(0, 0, c))
+    first_hops(0, 0, 1)
     for d in range(1, 4):
         go(remote(
             pbuf.at[x], pbuf.at[x], xs.at[d - 1], xr.at[d - 1], tap_of(y_hi, (x + d) % NX, z), b
         ))
-
-    step(0, 0)
+    first_hops(0, 2)
+
     remote(hp.at[x], hp.at[x], hs.at[0], hr.at[0], a, b_prev).wait_recv()
     go(remote(hp.at[x], hq.at[1, z], chs.at[0], chr_.at[0], far_tap, b))
     for d in range(1, 4):
         go(remote(
             hp.at[x], hp.at[x], xhs.at[d - 1], xhr.at[d - 1], tap_of(y_hi, (x + d) % NX, z), b
         ))
-    send_halos(0)
+    pass_on(0)
+    for c in range(2):
+        from_far(0, c)
+        first_hops(1, c)
+    first_hops(1, 2)
+    wait_for(0, 2)
+    go(later_halo(1))
+    go(later_halo(7))
     for d in range(1, 4):
         ref = pbuf.at[(x + NX - d) % NX]
         remote(ref, ref, xs.at[d - 1], xr.at[d - 1], z_up, b).wait_recv()
-    step(0, 1)
-    for c in range(2):
-        from_far(0, c)
-        go(up(1, 0, c))
-        go(down(1, 0, c))
     for d in range(1, 4):
         ref = hp.at[(x + NX - d) % NX]
         remote(ref, ref, xhs.at[d - 1], xhr.at[d - 1], z_up, b).wait_recv()
@@ -285,37 +304,40 @@
     for j in range(LEVELS):
         dq[0, j, ROWS : 2 * ROWS] = dp[j, own, :]
     remote(hq.at[1, z], hq.at[1, z], chs.at[0], chr_.at[0], far_tap, b).wait_recv()
-    send_halos(1)
+    for m in (2, 6, 1, 7, 3, 5, 4):
+        go(owner_halo(m))
+    columns(0, 2, 6)
     columns(0, 1, 7)
-    step(0, 2)
-    columns(0, 2, 6)
     product(0)
-    step(1, 0)
-    from_below(0, 3, 0)
-    go(far(4, 0))
-    from_above(0, 3, 1)
-    go(far(4, 1))
+    for c in range(2):
+        arrived(0, 1 - 2 * c, 5)
+        go(far(4, c))
+    go(later_halo(4))
+    wait_for(0, 3, 4)
+    go(later_halo(3))
+    go(later_halo(5))
+    pass_on(1)
     x_out(0)
+    wait_for(1, 2)
+    columns(1, 0, 2)
+    columns(1, 1, 7)
+    product(2)
     columns(0, 3, 5)
     columns(0, 4)
     product(1)
-    step(1, 1)
-    columns(1, 0, 1)
-    columns(1, 7, 2)
-    product(2)
+    x_out(2)
+    columns(1, 6)
+    y_out(0)
     x_out(1)
-    y_out(0)
-    columns(1, 6)
-    x_out(2)
-    step(1, 2)
+    wait_for(1, 3, 4)
     columns(1, 3, 5)
-    y_out(1)
     for c in range(2):
         from_far(4, c)
     columns(1, 4)
     product(3)
+    x_out(3)
     y_out(2)
-    x_out(3)
+    y_out(1)
     y_out(3)
 
     kind = jnp.where(y_lo // 2 == y_hi, 0, 2)
@@ -369,7 +391,7 @@
             pltpu.VMEM((CHUNKS, 2, LEVELS, ROWS, 128), f32),
             pltpu.VMEM((2, 3, LEVELS, ROWS, 128), f32),
             pltpu.SemaphoreType.DMA((1,)),
-            *sems(1, 3, 3, 4, 1, 16, 16, 14, CHUNKS, 3 * CHUNKS, 2 * CHUNKS),
+            *sems(1, 3, 3, 4, 1, 24, 7, 8, CHUNKS, 3 * CHUNKS, 2 * CHUNKS),
         ],
         compiler_params=pltpu.CompilerParams(
             collective_id=0, has_side_effects=True, vmem_limit_bytes=40 * 1024 * 1024

time: 50.1 us -> 47.6 us (0.950)
  Pallas kernels: 47.8 us -> 45.2 us
    pallas_call x1, Pallas kernels: 47.8 us -> 45.2 us  [body(): pl.pallas_call(kernel, out_shape=jax.ShapeDtypeStruct((LEVELS, ROWS, 256)...]
where the time goes in v4:
time: 47.6 us; the launch traced here: 47.4 us
  Pallas kernels  45.2 us (95%)
  local copies, waits for them, and re-layouts  2.16 us (5%)
    pallas_call x1, Pallas kernels, body(): pl.pallas_call(kernel, out_shape=jax.ShapeDtypeStruct((LEVELS, ROWS, 256)...  45.2 us
    unnamed x5, local copies, waits for them, and re-layouts  2.16 us

profile of v4, /device:TPU:25, one launch (start us, length us, event | category | flops | bytes accessed | tf_op | source)
XLA Modules:
  0.0 47.4 jit_solution(18140107657786206184)
XLA Ops:
  0.0 0.0 copy-start
  0.0 0.8 %copy-done = bf16[32,1024]{1,0:T(8,128)(2,1)S(1)} copy-done((bf16[32,1024]{1,0:T(8,128)(2,1)S(1)}, bf16[32,1024]{1,0:T(8,128)(2,1)}, u32[]{:S(2)}) %copy-start) | copy-done | bytes 65560
  0.8 0.0 copy-start.1
  0.8 0.7 %copy-done.1 = f32[2,16]{1,0:T(2,128)S(1)} copy-done((f32[2,16]{1,0:T(2,128)S(1)}, f32[2,16]{1,0:T(2,128)}, u32[]{:S(2)}) %copy-start.1) | copy-done | bytes 152
  1.5 45.2 %shard_map.28 = f32[3,32,256]{2,1,0:T(8,128)S(1)} custom-call(bf16[32,1024]{1,0:T(8,128)(2,1)S(1)} %copy-done, f32[2,16]{1,0:T(2,128)S(1)} %copy-done.1), custom_call_target="tpu_custom_call" | custom-call | flops 4000000000 | bytes 200000 | tf_op jit(solution)/shard_map/pallas_call | solution.py:372
  46.8 0.6 %copy.4 = f32[3,32,256]{2,1,0:T(8,128)} copy(f32[3,32,256]{2,1,0:T(8,128)S(1)} %shard_map.28) | data formatting | bytes 196608
Async XLA Ops:
  0.0 0.8 %copy-start = (bf16[32,1024]{1,0:T(8,128)(2,1)S(1)}, bf16[32,1024]{1,0:T(8,128)(2,1)}, u32[]{:S(2)}) copy-start(bf16[32,1024]{1,0:T(8,128)(2,1)} %p_ref.1) | copy-start | bytes 196612
  0.8 0.7 %copy-start.1 = (f32[2,16]{1,0:T(2,128)S(1)}, f32[2,16]{1,0:T(2,128)}, u32[]{:S(2)}) copy-start(f32[2,16]{1,0:T(2,128)} %f_ref.1) | copy-start | bytes 388

commit v5 on v4

--- a/solution.py
+++ b/solution.py
@@ -14,7 +14,7 @@
 WIN = 256
 OUT = 128
 NWIN = WIDTH // OUT
-SPLITS = 3
+SPLITS = 2
 LANES = 384
 CHUNKS = 4
 HALF = 16
@@ -70,8 +70,8 @@
 
 
 def kernel(
-    p_ref, f_ref, o_ref,
-    pbuf, hp, qbuf, hq, wbuf, dp, dq, part, sib, red, xo, yo,
+    p_ref, f_hbm, o_ref,
+    f_ref, pbuf, hp, qbuf, hq, wbuf, dp, dq, part, sib, red, xo, yo,
     ps, hs, hr, xs, xr, xhs, xhr, cs, cr, chs, chr_, zs, zr, zhs, zhr, ths, thr,
     ss, sr, xos, xor_, yos, yor,
 ):
@@ -95,6 +95,8 @@
 
     fetch = pltpu.make_async_copy(p_ref, pbuf.at[x], ps.at[0])
     fetch.start()
+    fetch_f = pltpu.make_async_copy(f_hbm, f_ref, ps.at[1])
+    fetch_f.start()
     barrier = pltpu.get_barrier_semaphore()
 
     def hello(tap, tm):
@@ -109,6 +111,7 @@
         hello(a, (b + 2 * d) % 8)
         hello(tap_of(y_hi, (x + d) % NX, z), b)
 
+    fetch_f.wait()
     build_bands(f_ref, wbuf)
     fetch.wait()
     pl.semaphore_wait(barrier, 16)
@@ -322,14 +325,14 @@
     columns(1, 0, 2)
     columns(1, 1, 7)
     product(2)
+    columns(1, 6)
+    x_out(2)
     columns(0, 3, 5)
     columns(0, 4)
     product(1)
-    x_out(2)
-    columns(1, 6)
     y_out(0)
+    wait_for(1, 3, 4)
     x_out(1)
-    wait_for(1, 3, 4)
     columns(1, 3, 5)
     for c in range(2):
         from_far(4, c)
@@ -340,28 +343,38 @@
     y_out(1)
     y_out(3)
 
+    def sent(q):
+        @pl.when(post)
+        def _():
+            for d in range(1, 4):
+                x_copy(q, d).wait_send()
+
+        pl.when(jnp.logical_not(post))(lambda: sib_copy(q).wait_send())
+
+    def y_sent(q):
+        for i in range(2):
+            pl.when(y_goal(q, i) != y_lo)(lambda: y_copy(q, i).wait_send())
+
+    for copy in sends:
+        copy.wait_send()
+    for q in range(CHUNKS):
+        sent(q)
+    for q in range(CHUNKS - 1):
+        y_sent(q)
+
     kind = jnp.where(y_lo // 2 == y_hi, 0, 2)
-    totals = []
+    turn = ((z + NZ - 1) % NZ) * ROWS
     for h in range(2):
         for d in range(1, 4):
             ref = yo.at[h, d - 1]
             remote(ref, ref, yos.at[0], yor.at[3 * h + d - 1], a, sibling).wait_recv()
-        totals.append(xo[kind + h, y_lo % 2] + yo[h, 0] + yo[h, 1] + yo[h, 2])
-    total = jnp.concatenate(totals, axis=2) * (1.0 / (WIDTH * 8))
+        if h == 0:
+            first = xo[kind, y_lo % 2] + yo[0, 0] + yo[0, 1] + yo[0, 2]
+    total = jnp.concatenate([first, xo[kind + 1, y_lo % 2] + yo[1, 0] + yo[1, 1] + yo[1, 2]], axis=2)
+    total = total * (1.0 / (WIDTH * 8))
     for j in range(LEVELS):
-        o_ref[j] = pltpu.roll(total[j], ((z + NZ - 1) % NZ) * ROWS, 1)
-
-    for copy in sends:
-        copy.wait_send()
-    for q in range(CHUNKS):
-        @pl.when(post)
-        def _():
-            for d in range(1, 4):
-                x_copy(q, d).wait_send()
-
-        pl.when(jnp.logical_not(post))(lambda: sib_copy(q).wait_send())
-        for i in range(2):
-            pl.when(y_goal(q, i) != y_lo)(lambda: y_copy(q, i).wait_send())
+        o_ref[j] = pltpu.roll(total[j], turn, 1)
+    y_sent(CHUNKS - 1)
 
 
 def body(pressure, filters):
@@ -374,10 +387,11 @@
         out_shape=jax.ShapeDtypeStruct((LEVELS, ROWS, 256), f32),
         in_specs=[
             pl.BlockSpec(memory_space=pltpu.HBM),
-            pl.BlockSpec(memory_space=pltpu.SMEM),
+            pl.BlockSpec(memory_space=pltpu.HBM),
         ],
         out_specs=pl.BlockSpec(memory_space=pltpu.VMEM),
         scratch_shapes=[
+            pltpu.SMEM((2, FILT), f32),
             pltpu.VMEM((NX, ROWS, WIDTH), bf16),
             pltpu.VMEM((NX, ROWS, HALO), bf16),
             pltpu.VMEM((2, NZ, ROWS, WIDTH), bf16),
@@ -390,11 +404,11 @@
             pltpu.VMEM((CHUNKS, NX, LEVELS, ROWS, 128), f32),
             pltpu.VMEM((CHUNKS, 2, LEVELS, ROWS, 128), f32),
             pltpu.VMEM((2, 3, LEVELS, ROWS, 128), f32),
-            pltpu.SemaphoreType.DMA((1,)),
+            pltpu.SemaphoreType.DMA((2,)),
             *sems(1, 3, 3, 4, 1, 24, 7, 8, CHUNKS, 3 * CHUNKS, 2 * CHUNKS),
         ],
         compiler_params=pltpu.CompilerParams(
-            collective_id=0, has_side_effects=True, vmem_limit_bytes=40 * 1024 * 1024
+            collective_id=0, has_side_effects=True, vmem_limit_bytes=63 * 1024 * 1024
         ),
         cost_estimate=pl.CostEstimate(
             flops=4_000_000_000, bytes_accessed=200_000, transcendentals=0

time: 47.6 us -> 46.6 us (0.979)
  local copies, waits for them, and re-layouts: 2.16 us -> 1.54 us
    unnamed x5 -> x1, local copies, waits for them, and re-layouts: 2.16 us -> 1.54 us
where the time goes in v5:
time: 46.6 us; the launch traced here: 46.4 us
  Pallas kernels  44.9 us (96%)
  local copies, waits for them, and re-layouts  1.54 us (3%)
    pallas_call x1, Pallas kernels, body(): pl.pallas_call(kernel, out_shape=jax.ShapeDtypeStruct((LEVELS, ROWS, 256)...  44.9 us
    unnamed x1, local copies, waits for them, and re-layouts  1.54 us

profile of v5, /device:TPU:25, one launch (start us, length us, event | category | flops | bytes accessed | tf_op | source)
XLA Modules:
  0.0 46.4 jit_solution(11810540985386651623)
XLA Ops:
  0.0 44.9 %shard_map.28 = f32[3,32,256]{2,1,0:T(8,128)} custom-call(bf16[32,1024]{1,0:T(8,128)(2,1)} %p_ref.1, f32[2,16]{1,0:T(2,128)} %f_hbm.1), custom_call_target="tpu_custom_call" | custom-call | flops 4000000000 | bytes 200000 | tf_op jit(solution)/shard_map/pallas_call | solution.py:385
  44.9 1.5 %copy.4 = f32[3,32,256]{2,1,0:T(8,128)} copy(f32[3,32,256]{2,1,0:T(8,128)} %shard_map.28) | data formatting | bytes 196608

commit v6 on v5

--- a/solution.py
+++ b/solution.py
@@ -217,30 +217,45 @@
                         val[first : first + ROWS, j * OUT : (j + 1) * OUT]
                     )
 
-    def sib_copy(q):
-        return remote(part.at[q], sib.at[q], ss.at[q], sr.at[q], a, sibling)
+    def parts(q):
+        return range(LEVELS) if q == CHUNKS - 1 else (None,)
+
+    def pick(ref, j):
+        return ref if j is None else ref.at[j]
+
+    def sib_copy(q, j):
+        n = q + (j or 0)
+        return remote(
+            pick(part.at[q], j), pick(sib.at[q], j), ss.at[n], sr.at[n], a, sibling
+        )
 
     def product(q):
         for j in range(LEVELS):
             part[q, j] = lax.dot_general(dp[j], dq[q, j], NT, preferred_element_type=jnp.float32)
-        pl.when(jnp.logical_not(post))(lambda: sib_copy(q).start())
-
-    def x_copy(q, d):
+            if j in parts(q):
+                pl.when(jnp.logical_not(post))(lambda: sib_copy(q, j).start())
+        if None in parts(q):
+            pl.when(jnp.logical_not(post))(lambda: sib_copy(q, None).start())
+
+    def x_copy(q, j, d):
         there = (x + d) % NX
-        return remote(
-            red.at[q, there], xo.at[q, x // 2], xos.at[3 * q + d - 1], xor_.at[2 * q + x // 2],
-            tap_of(y_hi, there, z), b,
+        n = q + (j or 0)
+        return remote(
+            pick(red.at[q, there], j), pick(xo.at[q, x // 2], j),
+            xos.at[3 * n + d - 1], xor_.at[2 * n + x // 2], tap_of(y_hi, there, z), b,
         )
 
     def x_out(q):
         @pl.when(post)
         def _():
-            sib_copy(q).wait_recv()
-            for i in range(NX):
-                rows = slice(i * ROWS, (i + 1) * ROWS)
-                red[q, i] = part[q, :, rows] + sib[q, :, rows]
-            for d in (2, 1, 3):
-                x_copy(q, d).start()
+            for j in parts(q):
+                sib_copy(q, j).wait_recv()
+                for i in range(NX):
+                    rows = slice(i * ROWS, (i + 1) * ROWS)
+                    for level in range(LEVELS) if j is None else (j,):
+                        red[q, i, level] = part[q, level, rows] + sib[q, level, rows]
+                for d in (2, 1, 3):
+                    x_copy(q, j, d).start()
             xo[q, x // 2] = red[q, x]
 
     def y_goal(q, i):
@@ -258,8 +273,10 @@
         for i in range(2):
             @pl.when(2 * i + core != x)
             def _():
-                ref = xo.at[q, i]
-                remote(ref, ref, xos.at[0], xor_.at[2 * q + i], z_up, b).wait_recv()
+                for j in parts(q):
+                    ref = pick(xo.at[q, i], j)
+                    n = q + (j or 0)
+                    remote(ref, ref, xos.at[0], xor_.at[2 * n + i], z_up, b).wait_recv()
 
             pl.when(y_goal(q, i) != y_lo)(lambda: y_copy(q, i).start())
 
@@ -346,10 +363,12 @@
     def sent(q):
         @pl.when(post)
         def _():
-            for d in range(1, 4):
-                x_copy(q, d).wait_send()
-
-        pl.when(jnp.logical_not(post))(lambda: sib_copy(q).wait_send())
+            for j in parts(q):
+                for d in range(1, 4):
+                    x_copy(q, j, d).wait_send()
+
+        for j in parts(q):
+            pl.when(jnp.logical_not(post))(lambda: sib_copy(q, j).wait_send())
 
     def y_sent(q):
         for i in range(2):
@@ -405,7 +424,7 @@
             pltpu.VMEM((CHUNKS, 2, LEVELS, ROWS, 128), f32),
             pltpu.VMEM((2, 3, LEVELS, ROWS, 128), f32),
             pltpu.SemaphoreType.DMA((2,)),
-            *sems(1, 3, 3, 4, 1, 24, 7, 8, CHUNKS, 3 * CHUNKS, 2 * CHUNKS),
+            *sems(1, 3, 3, 4, 1, 24, 7, 8, CHUNKS + 2, 3 * CHUNKS + 6, 2 * CHUNKS + 4),
         ],
         compiler_params=pltpu.CompilerParams(
             collective_id=0, has_side_effects=True, vmem_limit_bytes=63 * 1024 * 1024

time: 46.6 us -> 47 us (level)
  no operation moved by 1% of the time
where the time goes in v6:
time: 47 us; the launch traced here: 46.8 us
  Pallas kernels  45.3 us (96%)
  local copies, waits for them, and re-layouts  1.54 us (3%)
    pallas_call x1, Pallas kernels, body(): pl.pallas_call(kernel, out_shape=jax.ShapeDtypeStruct((LEVELS, ROWS, 256)...  45.3 us
    unnamed x1, local copies, waits for them, and re-layouts  1.54 us

profile of v6, /device:TPU:25, one launch (start us, length us, event | category | flops | bytes accessed | tf_op | source)
XLA Modules:
  0.0 46.8 jit_solution(94907429630541063)
XLA Ops:
  0.0 45.3 %shard_map.28 = f32[3,32,256]{2,1,0:T(8,128)} custom-call(bf16[32,1024]{1,0:T(8,128)(2,1)} %p_ref.1, f32[2,16]{1,0:T(2,128)} %f_hbm.1), custom_call_target="tpu_custom_call" | custom-call | flops 4000000000 | bytes 200000 | tf_op jit(solution)/shard_map/pallas_call | solution.py:404
  45.3 1.5 %copy.4 = f32[3,32,256]{2,1,0:T(8,128)} copy(f32[3,32,256]{2,1,0:T(8,128)} %shard_map.28) | data formatting | bytes 196608
